TPU v7x, 32 devices: a whole 2x2x4 slice. The times are simulated.
32 devices in a mesh: vel: 4 (over x, core), sx: 2 (over y), sy: 4 (over z).
Axes of the slice: x: 2, y: 2, z: 4, core: 2. Of those that a mesh axis runs over, the one named last changes fastest.
Arguments:
- distribution: bfloat16 [6, 128, 32768], P('sx', 'sy', 'vel'), may hold values from 0.05 to 5, as said below
- plane_weights: bfloat16 [1024, 1024], P(('sx', 'sy')), may hold values from -0.1875 to 0.1875
- depth_weights: bfloat16 [32, 32], replicated, may hold values from -1 to 1
Outputs:
- advanced: bfloat16 [6, 128, 32768], P('sx', 'sy', 'vel')
Inputs may be any that keep to these rules, and one draw needn't show every extreme that they name: `distribution`: every entry is positive.
All inputs are finite; a program needn't handle non-finite values.
Results may differ from a plain program's by a relative error of at most 0.0028.
Values may be sent and summed in bfloat16 or wider, within the bound.
A program may use at most 64 MiB of HBM per device.

v0:
```python
import functools
import math

import jax
import jax.numpy as jnp
from jax import lax
from jax.experimental import pallas as pl
from jax.experimental.pallas import tpu as pltpu
from jax.sharding import PartitionSpec as P

NVZ = 32
NVX = 32
NVY = 32
NXY = NVX * NVY
HALF = NXY // 2
GROUP = 16
COURANT = 0.45
RELAX_RATE = 0.3
MESH = pl.DeviceIdType.MESH
F32 = jnp.float32
BF16 = jnp.bfloat16


def lane_speeds(shape, dim):
    lane = lax.broadcasted_iota(jnp.int32, shape, dim)
    across = ((lane >> 5).astype(F32) - (NVX - 1) / 2.0) * (8.0 / NVX)
    along = ((lane & 31).astype(F32) - (NVY - 1) / 2.0) * (8.0 / NVY)
    return across, along


def kernel(
    sizes, f_hbm, w_hbm, d_ref, out_hbm,
    tiles, weights, base, mixed, result, spread, probes,
    row_out, row_in, col_out, col_in, col_wide,
    loc_sem, wloc_sem, x_send, x_recv, sib_send, sib_recv, fw_send, fw_recv,
    w_send, w_recv, wf_sem, halo_send, halo_recv, out_sem,
):
    nvel, nsx, nsy = sizes
    nh = nvel // 2
    peers = nsx * nsy
    tile_rows, tile_cols, _ = f_hbm.shape
    depth = NVZ // nvel
    per_row = tile_cols // GROUP
    chunks = tile_rows * per_row
    share = NXY // peers
    vel = lax.axis_index("vel")
    sx = lax.axis_index("sx")
    sy = lax.axis_index("sy")
    high, low = lax.div(vel, 2), lax.rem(vel, 2)
    sibling = high * 2 + 1 - low
    me = sx * nsy + sy

    barrier = pltpu.get_barrier_semaphore()

    def greet(i, carry):
        peer = lax.rem(me + i, peers)
        pl.semaphore_signal(
            barrier, inc=1,
            device_id={"sx": lax.div(peer, nsy), "sy": lax.rem(peer, nsy)},
            device_id_type=MESH,
        )
        return carry

    for i in range(1, nh):
        pl.semaphore_signal(
            barrier, inc=1, device_id={"vel": lax.rem(high + i, nh) * 2 + low},
            device_id_type=MESH,
        )
    pl.semaphore_signal(barrier, inc=1, device_id={"vel": sibling}, device_id_type=MESH)
    lax.fori_loop(1, peers, greet, 0)

    def piece(k):
        return f_hbm.at[
            k // per_row, pl.ds(pl.multiple_of((k % per_row) * GROUP, GROUP), GROUP), :
        ]

    half_lanes = pl.ds(pl.multiple_of(low * HALF, HALF), HALF)
    sib_lanes = pl.ds(pl.multiple_of((1 - low) * HALF, HALF), HALF)

    def share_rows(owner):
        return pl.ds(pl.multiple_of(owner * share, share), share)

    def load_own(k):
        return pltpu.make_async_copy(piece(k), tiles.at[vel, k], loc_sem.at[k])

    own_weights = pltpu.make_async_copy(
        w_hbm.at[:, half_lanes], weights.at[share_rows(me), half_lanes], wloc_sem
    )
    for k in range(chunks):
        load_own(k).start()
    own_weights.start()
    pl.semaphore_wait(barrier, peers + nh - 1)

    def to_chip(k, i):
        other = lax.rem(high + i, nh)
        return pltpu.make_async_remote_copy(
            src_ref=piece(k), dst_ref=tiles.at[vel, k],
            send_sem=x_send.at[other, k], recv_sem=x_recv.at[high, k],
            device_id={"vel": other * 2 + low}, device_id_type=MESH,
        )

    def from_chip(k, i):
        other = lax.rem(high + i, nh)
        return pltpu.make_async_remote_copy(
            src_ref=piece(k), dst_ref=tiles.at[other * 2 + low, k],
            send_sem=x_send.at[other, k], recv_sem=x_recv.at[other, k],
            device_id={"vel": other * 2 + low}, device_id_type=MESH,
        )

    def to_sibling(k):
        return pltpu.make_async_remote_copy(
            src_ref=piece(k), dst_ref=tiles.at[vel, k],
            send_sem=sib_send.at[k], recv_sem=sib_recv.at[k],
            device_id={"vel": sibling}, device_id_type=MESH,
        )

    def from_sibling(k):
        return pltpu.make_async_remote_copy(
            src_ref=piece(k), dst_ref=tiles.at[sibling, k],
            send_sem=sib_send.at[k], recv_sem=sib_recv.at[k],
            device_id={"vel": sibling}, device_id_type=MESH,
        )

    def forward(k, i):
        other = lax.rem(high + i, nh)
        slot = other * 2 + low
        return pltpu.make_async_remote_copy(
            src_ref=tiles.at[slot, k], dst_ref=tiles.at[slot, k],
            send_sem=fw_send.at[other, k], recv_sem=fw_recv.at[other, k],
            device_id={"vel": sibling}, device_id_type=MESH,
        )

    def forwarded(k, i):
        other = lax.rem(high + i, nh)
        slot = other * 2 + 1 - low
        return pltpu.make_async_remote_copy(
            src_ref=tiles.at[slot, k], dst_ref=tiles.at[slot, k],
            send_sem=fw_send.at[other, k], recv_sem=fw_recv.at[other, k],
            device_id={"vel": sibling}, device_id_type=MESH,
        )

    def send_weights(i):
        peer = lax.rem(me + i, peers)
        return pltpu.make_async_remote_copy(
            src_ref=w_hbm.at[:, half_lanes], dst_ref=weights.at[share_rows(me), half_lanes],
            send_sem=w_send.at[peer], recv_sem=w_recv.at[me],
            device_id={"sx": lax.div(peer, nsy), "sy": lax.rem(peer, nsy)},
            device_id_type=MESH,
        )

    def take_weights(i):
        peer = lax.rem(me + i, peers)
        return pltpu.make_async_remote_copy(
            src_ref=w_hbm.at[:, half_lanes], dst_ref=weights.at[share_rows(peer), half_lanes],
            send_sem=w_send.at[peer], recv_sem=w_recv.at[peer],
            device_id={"sx": lax.div(peer, nsy), "sy": lax.rem(peer, nsy)},
            device_id_type=MESH,
        )

    def swap_weights(lanes):
        return pltpu.make_async_remote_copy(
            src_ref=weights.at[:, lanes], dst_ref=weights.at[:, lanes],
            send_sem=wf_sem.at[0], recv_sem=wf_sem.at[1],
            device_id={"vel": sibling}, device_id_type=MESH,
        )

    def row_halo(way):
        target = lax.rem(sx + (1 if way == 0 else nsx - 1), nsx)
        return pltpu.make_async_remote_copy(
            src_ref=row_out.at[way], dst_ref=row_in.at[way],
            send_sem=halo_send.at[way], recv_sem=halo_recv.at[way],
            device_id={"sx": target}, device_id_type=MESH,
        )

    def col_halo(way):
        target = lax.rem(sy + (1 if way == 0 else nsy - 1), nsy)
        return pltpu.make_async_remote_copy(
            src_ref=col_out.at[way], dst_ref=col_in.at[way],
            send_sem=halo_send.at[2 + way], recv_sem=halo_recv.at[2 + way],
            device_id={"sy": target}, device_id_type=MESH,
        )

    for k in range(chunks):
        for i in range(1, nh):
            to_chip(k, i).start()
        to_sibling(k).start()

    def start_weights(i, carry):
        send_weights(i).start()
        return carry

    lax.fori_loop(1, peers, start_weights, 0)

    for k in range(chunks):
        load_own(k).wait()

    for z in range(depth):
        for j in range(per_row):
            rows = slice(j * GROUP, (j + 1) * GROUP)
            lanes = slice(z * HALF, (z + 1) * HALF)
            row_out[0, rows, lanes] = tiles[
                vel, (tile_rows - 1) * per_row + j, :, z * NXY + HALF:(z + 1) * NXY
            ]
            row_out[1, rows, lanes] = tiles[vel, j, :, z * NXY:z * NXY + HALF]
    row_halo(0).start()
    row_halo(1).start()
    packed = col_out.shape[1]
    edge = depth * tile_rows * GROUP
    for way, (part, line) in enumerate(((per_row - 1, GROUP - 1), (0, 0))):
        stack = jnp.concatenate(
            [
                tiles[vel, r * per_row + part, :, z * NXY:(z + 1) * NXY]
                for r in range(tile_rows)
                for z in range(depth)
            ],
            axis=0,
        )
        pick = (
            lax.broadcasted_iota(jnp.int32, (packed, edge), 1)
            == lax.broadcasted_iota(jnp.int32, (packed, edge), 0) * GROUP + line
        )
        pick = jnp.where(pick, 1.0, 0.0).astype(BF16)
        col_out[way] = jnp.dot(pick, stack, preferred_element_type=F32).astype(BF16)
        col_halo(way).start()

    rows, cols = spread.shape
    first = vel * depth
    chosen = (
        lax.broadcasted_iota(jnp.int32, (rows, NVZ), 1)
        == (lax.broadcasted_iota(jnp.int32, (rows, NVZ), 0) >> 4) + first
    )
    fan = (
        lax.broadcasted_iota(jnp.int32, (NVZ, cols), 0)
        == lax.broadcasted_iota(jnp.int32, (NVZ, cols), 1) >> 4
    )
    own = jnp.dot(
        jnp.where(chosen, 1.0, 0.0).astype(BF16), d_ref[...], preferred_element_type=F32
    ).astype(BF16)
    wide = jnp.dot(own, jnp.where(fan, 1.0, 0.0).astype(BF16), preferred_element_type=F32)
    same = (
        lax.broadcasted_iota(jnp.int32, (rows, cols), 0) & (GROUP - 1)
    ) == (lax.broadcasted_iota(jnp.int32, (rows, cols), 1) & (GROUP - 1))
    spread[...] = jnp.where(same, wide, 0.0).astype(BF16)

    across, along = lane_speeds((NXY, 128), 0)
    column = lax.broadcasted_iota(jnp.int32, (NXY, 128), 1)
    square = across * across + along * along
    coarse = square.astype(BF16).astype(F32)
    probe = jnp.where(column == 0, 1.0, 0.0)
    probe = jnp.where(column == 1, across, probe)
    probe = jnp.where(column == 2, along, probe)
    probe = jnp.where(column == 3, coarse, probe)
    probe = jnp.where(column == 4, square - coarse, probe)
    probes[...] = probe.astype(BF16)

    vz = [(w - (NVZ - 1) / 2.0) * (8.0 / NVZ) for w in range(NVZ)]

    def relax(k):
        stack = jnp.concatenate(
            [
                tiles[v, k, :, z * NXY:(z + 1) * NXY]
                for v in range(nvel)
                for z in range(depth)
            ],
            axis=0,
        )
        sums = jnp.dot(stack, probes[...], preferred_element_type=F32)
        plain = jnp.zeros((GROUP, 128), F32)
        first_order = jnp.zeros((GROUP, 128), F32)
        second_order = jnp.zeros((GROUP, 128), F32)
        for w in range(NVZ):
            term = sums[w * GROUP:(w + 1) * GROUP]
            plain = plain + term
            first_order = first_order + vz[w] * term
            second_order = second_order + (vz[w] * vz[w]) * term

        def lanes(block, q):
            return jnp.broadcast_to(block[:, q:q + 1], (GROUP, 128))

        density = lanes(plain, 0)
        ux = lanes(plain, 1) / density
        uy = lanes(plain, 2) / density
        uz = lanes(first_order, 0) / density
        energy = lanes(plain, 3) + lanes(plain, 4) + lanes(second_order, 0)
        heat = (energy / density - (ux * ux + uy * uy + uz * uz)) / 3.0
        spread_heat = (2.0 * math.pi) * heat
        volume = (8.0 / NVX) * (8.0 / NVY) * (8.0 / NVZ)
        scale = density * volume / (spread_heat * jnp.sqrt(spread_heat))
        rate = 0.5 / heat

        def wider(block, count):
            return jnp.concatenate([block] * count, axis=1)

        vx, vy = lane_speeds((GROUP, NXY), 1)
        gap_x = vx - wider(ux, NXY // 128)
        gap_y = vy - wider(uy, NXY // 128)
        plane = jnp.exp(-(gap_x * gap_x + gap_y * gap_y) * wider(rate, NXY // 128))
        column = jnp.concatenate(
            [scale * jnp.exp(-((vz[w] - uz) * (vz[w] - uz)) * rate) for w in range(NVZ)], axis=0
        )
        head = column.astype(BF16)
        rest = (column - head.astype(F32)).astype(BF16)
        depth_mix = jnp.dot(spread[...], head, preferred_element_type=F32) + jnp.dot(
            spread[...], rest, preferred_element_type=F32
        )
        mix = jnp.dot(spread[...], stack, preferred_element_type=F32)
        even = wider(depth_mix, NXY // 128) * jnp.concatenate([plane] * depth, axis=0)
        mixed[k] = (even - mix).astype(BF16)

    vx, vy = lane_speeds((1, NXY), 1)
    pace_x, pace_y = jnp.abs(vx), jnp.abs(vy)
    toward = vy > 0.0

    def transport():
        for way in range(2):
            row_halo(way).wait_recv()
            col_halo(way).wait_recv()
        col_wide[...] = col_in[...].astype(F32)
        line = lax.broadcasted_iota(jnp.int32, (tile_cols, NXY), 0)
        for r in range(tile_rows):

            def plane_step(z, carry):
                whole = pl.ds(pl.multiple_of(z * NXY, NXY), NXY)
                left_half = pl.ds(pl.multiple_of(z * NXY, HALF), HALF)
                right_half = pl.ds(pl.multiple_of(z * NXY + HALF, HALF), HALF)
                packed_half = pl.ds(pl.multiple_of(z * HALF, HALF), HALF)

                def row(index, lanes):
                    return jnp.concatenate(
                        [tiles[vel, index * per_row + j, :, lanes] for j in range(per_row)],
                        axis=0,
                    ).astype(F32)

                current = row(r, whole)
                place = pl.ds(r * depth + z, 1)
                left = jnp.where(line == 0, col_wide[0, place, :], pltpu.roll(current, 1, 0))
                right = jnp.where(
                    line == tile_cols - 1,
                    col_wide[1, place, :],
                    pltpu.roll(current, tile_cols - 1, 0),
                )
                if r == tile_rows - 1:
                    upper = row_in[1, :, packed_half].astype(F32)
                else:
                    upper = row(r + 1, left_half)
                if r == 0:
                    lower = row_in[0, :, packed_half].astype(F32)
                else:
                    lower = row(r - 1, right_half)
                across = pace_x * (current - jnp.concatenate([upper, lower], axis=1))
                along = pace_y * (current - jnp.where(toward, left, right))
                moved = current - (
                    COURANT / (4.0 - 4.0 / NVX) * across + COURANT / (4.0 - 4.0 / NVY) * along
                )
                for j in range(per_row):
                    base[r * per_row + j, :, whole] = moved[j * GROUP:(j + 1) * GROUP]
                return carry

            lax.fori_loop(0, depth, plane_step, 0)

    def store(k):
        return pltpu.make_async_copy(
            result.at[k],
            out_hbm.at[
                k // per_row, pl.ds(pl.multiple_of((k % per_row) * GROUP, GROUP), GROUP), :
            ],
            out_sem.at[k],
        )

    def finish(k, carry):
        collision = lax.dot_general(
            mixed[k], weights[...], (((1,), (1,)), ((), ())), preferred_element_type=F32
        )
        for z in range(depth):
            lanes = slice(z * NXY, (z + 1) * NXY)
            result[k, :, lanes] = (
                base[k, :, lanes] + RELAX_RATE * collision[z * GROUP:(z + 1) * GROUP]
            ).astype(BF16)
        store(k).start()
        return carry

    gate = chunks - 1

    def step(k, carry):
        for i in range(1, nh):
            from_chip(k, i).wait_recv()
            forward(k, i).start()
        from_sibling(k).wait_recv()
        for i in range(1, nh):
            forwarded(k, i).wait_recv()
        relax(k)

        @pl.when(k == chunks - 2)
        def _():
            own_weights.wait()

            def take(i, c):
                take_weights(i).wait_recv()
                return c

            lax.fori_loop(1, peers, take, 0)
            swap_weights(half_lanes).start()

        @pl.when(k == 2)
        def _():
            transport()

        @pl.when(k == gate)
        def _():
            swap_weights(sib_lanes).wait_recv()

        lax.fori_loop(
            jnp.where(k == gate, 0, k), jnp.where(k >= gate, k + 1, k), finish, 0
        )
        return carry

    lax.fori_loop(0, chunks, step, 0)

    for k in range(chunks):
        for i in range(1, nh):
            to_chip(k, i).wait_send()
            forward(k, i).wait_send()
        to_sibling(k).wait_send()
        store(k).wait()

    def sent(i, carry):
        send_weights(i).wait_send()
        return carry

    lax.fori_loop(1, peers, sent, 0)
    swap_weights(half_lanes).wait_send()
    for way in range(2):
        row_halo(way).wait_send()
        col_halo(way).wait_send()


def local(sizes, distribution, plane_weights, depth_weights):
    nvel, nsx, nsy = sizes
    tile_rows, tile_cols, width = distribution.shape
    depth = width // NXY
    chunks = tile_rows * tile_cols // GROUP
    packed = -(-tile_rows * depth // 16) * 16
    dma = pltpu.SemaphoreType.DMA
    cells = tile_rows * tile_cols
    return pl.pallas_call(
        functools.partial(kernel, sizes),
        out_shape=jax.ShapeDtypeStruct(distribution.shape, BF16),
        in_specs=[
            pl.BlockSpec(memory_space=pl.ANY),
            pl.BlockSpec(memory_space=pl.ANY),
            pl.BlockSpec(memory_space=pltpu.VMEM),
        ],
        out_specs=pl.BlockSpec(memory_space=pl.ANY),
        scratch_shapes=[
            pltpu.VMEM((nvel, chunks, GROUP, width), BF16),
            pltpu.VMEM((NXY, NXY), BF16),
            pltpu.VMEM((chunks, GROUP, width), F32),
            pltpu.VMEM((chunks, GROUP * depth, NXY), BF16),
            pltpu.VMEM((chunks, GROUP, width), BF16),
            pltpu.VMEM((GROUP * depth, GROUP * NVZ), BF16),
            pltpu.VMEM((NXY, 128), BF16),
            pltpu.VMEM((2, tile_cols, depth * HALF), BF16),
            pltpu.VMEM((2, tile_cols, depth * HALF), BF16),
            pltpu.VMEM((2, packed, NXY), BF16),
            pltpu.VMEM((2, packed, NXY), BF16),
            pltpu.VMEM((2, packed, NXY), F32),
            dma((chunks,)),
            dma,
            dma((nvel // 2, chunks)),
            dma((nvel // 2, chunks)),
            dma((chunks,)),
            dma((chunks,)),
            dma((nvel // 2, chunks)),
            dma((nvel // 2, chunks)),
            dma((nsx * nsy,)),
            dma((nsx * nsy,)),
            dma((2,)),
            dma((4,)),
            dma((4,)),
            dma((chunks,)),
        ],
        compiler_params=pltpu.CompilerParams(
            collective_id=0, has_side_effects=True, vmem_limit_bytes=56 * 1024 * 1024
        ),
        cost_estimate=pl.CostEstimate(
            flops=2 * cells * depth * NXY * NXY,
            bytes_accessed=4 * cells * width,
            transcendentals=cells * NXY,
        ),
    )(distribution, plane_weights, depth_weights)


def solution(mesh):
    sizes = (mesh.shape["vel"], mesh.shape["sx"], mesh.shape["sy"])
    return jax.shard_map(
        functools.partial(local, sizes),
        mesh=mesh,
        in_specs=(P("sx", "sy", "vel"), P(("sx", "sy"), None), P()),
        out_specs=P("sx", "sy", "vel"),
        check_vma=False,
    )
```

profile of v0, /device:TPU:0, one launch (start us, length us, event | category | flops | bytes accessed | tf_op | source)
XLA Modules:
  0.0 54.0 jit_solution(5788806715072770192)
XLA Ops:
  0.0 51.4 %shard_map.37 = bf16[3,32,8192]{2,1,0:T(8,128)(2,1)} custom-call(bf16[3,32,8192]{2,1,0:T(8,128)(2,1)} %f_hbm.1, bf16[128,1024]{1,0:T(8,128)(2,1)} %w_hbm.1, bf16[32,32]{1,0:T(8,128)(2,1)} %d_ref.1), custom_call_target="tpu_custom_call" | custom-call | flops 1610612736 | bytes 3145728 | tf_op jit(solution)/shard_map/pallas_call | solution.py:445
  51.4 2.7 %copy.5 = bf16[3,32,8192]{2,1,0:T(8,128)(2,1)} copy(bf16[3,32,8192]{2,1,0:T(8,128)(2,1)} %shard_map.37) | data formatting | bytes 3145728
where the time goes:
time: 54.3 us; the launch traced here: 54 us
  Pallas kernels  51.4 us (95%)
  local copies, waits for them, and re-layouts  2.65 us (5%)
    pallas_call x1, Pallas kernels, local(): pl.pallas_call(functools.partial(kernel, sizes), out_shape=jax.ShapeDtype...  51.4 us
    unnamed x1, local copies, waits for them, and re-layouts  2.65 us

commit v1 on v0

--- a/solution.py
+++ b/solution.py
@@ -30,9 +30,10 @@
 
 def kernel(
     sizes, f_hbm, w_hbm, d_ref, out_hbm,
-    tiles, weights, base, mixed, result, spread, probes,
+    own, tiles, weights, base, mixed, result, spread, probes, near_mix, near_sums,
+    back_out, back_in,
     row_out, row_in, col_out, col_in, col_wide,
-    loc_sem, wloc_sem, x_send, x_recv, sib_send, sib_recv, fw_send, fw_recv,
+    loc_sem, part_sem, wloc_sem, x_send, x_recv, back_send, back_recv,
     w_send, w_recv, wf_sem, halo_send, halo_recv, out_sem,
 ):
     nvel, nsx, nsy = sizes
@@ -61,12 +62,10 @@
         )
         return carry
 
-    for i in range(1, nh):
+    for i in range(1, nvel):
         pl.semaphore_signal(
-            barrier, inc=1, device_id={"vel": lax.rem(high + i, nh) * 2 + low},
-            device_id_type=MESH,
-        )
-    pl.semaphore_signal(barrier, inc=1, device_id={"vel": sibling}, device_id_type=MESH)
+            barrier, inc=1, device_id={"vel": lax.rem(vel + i, nvel)}, device_id_type=MESH
+        )
     lax.fori_loop(1, peers, greet, 0)
 
     def piece(k):
@@ -74,6 +73,9 @@
             k // per_row, pl.ds(pl.multiple_of((k % per_row) * GROUP, GROUP), GROUP), :
         ]
 
+    def cells_of(r, core):
+        return f_hbm.at[r, pl.ds(pl.multiple_of(core * GROUP, GROUP), GROUP), :]
+
     half_lanes = pl.ds(pl.multiple_of(low * HALF, HALF), HALF)
     sib_lanes = pl.ds(pl.multiple_of((1 - low) * HALF, HALF), HALF)
 
@@ -81,61 +83,43 @@
         return pl.ds(pl.multiple_of(owner * share, share), share)
 
     def load_own(k):
-        return pltpu.make_async_copy(piece(k), tiles.at[vel, k], loc_sem.at[k])
+        return pltpu.make_async_copy(piece(k), own.at[k], loc_sem.at[k])
+
+    def load_part(r):
+        return pltpu.make_async_copy(
+            cells_of(r, low), tiles.at[low, r], part_sem.at[r]
+        )
 
     own_weights = pltpu.make_async_copy(
         w_hbm.at[:, half_lanes], weights.at[share_rows(me), half_lanes], wloc_sem
     )
     for k in range(chunks):
         load_own(k).start()
+    for r in range(tile_rows):
+        load_part(r).start()
     own_weights.start()
-    pl.semaphore_wait(barrier, peers + nh - 1)
-
-    def to_chip(k, i):
-        other = lax.rem(high + i, nh)
-        return pltpu.make_async_remote_copy(
-            src_ref=piece(k), dst_ref=tiles.at[vel, k],
-            send_sem=x_send.at[other, k], recv_sem=x_recv.at[high, k],
-            device_id={"vel": other * 2 + low}, device_id_type=MESH,
-        )
-
-    def from_chip(k, i):
-        other = lax.rem(high + i, nh)
-        return pltpu.make_async_remote_copy(
-            src_ref=piece(k), dst_ref=tiles.at[other * 2 + low, k],
-            send_sem=x_send.at[other, k], recv_sem=x_recv.at[other, k],
-            device_id={"vel": other * 2 + low}, device_id_type=MESH,
-        )
-
-    def to_sibling(k):
-        return pltpu.make_async_remote_copy(
-            src_ref=piece(k), dst_ref=tiles.at[vel, k],
-            send_sem=sib_send.at[k], recv_sem=sib_recv.at[k],
-            device_id={"vel": sibling}, device_id_type=MESH,
-        )
-
-    def from_sibling(k):
-        return pltpu.make_async_remote_copy(
-            src_ref=piece(k), dst_ref=tiles.at[sibling, k],
-            send_sem=sib_send.at[k], recv_sem=sib_recv.at[k],
-            device_id={"vel": sibling}, device_id_type=MESH,
-        )
-
-    def forward(k, i):
-        other = lax.rem(high + i, nh)
-        slot = other * 2 + low
-        return pltpu.make_async_remote_copy(
-            src_ref=tiles.at[slot, k], dst_ref=tiles.at[slot, k],
-            send_sem=fw_send.at[other, k], recv_sem=fw_recv.at[other, k],
-            device_id={"vel": sibling}, device_id_type=MESH,
-        )
-
-    def forwarded(k, i):
-        other = lax.rem(high + i, nh)
-        slot = other * 2 + 1 - low
-        return pltpu.make_async_remote_copy(
-            src_ref=tiles.at[slot, k], dst_ref=tiles.at[slot, k],
-            send_sem=fw_send.at[other, k], recv_sem=fw_recv.at[other, k],
+    pl.semaphore_wait(barrier, peers + nvel - 2)
+
+    def give(r, i, core):
+        return pltpu.make_async_remote_copy(
+            src_ref=cells_of(r, core),
+            dst_ref=tiles.at[lax.rem(nh - i, nh) * 2 + low, r],
+            send_sem=x_send.at[i * 2 + core, r],
+            recv_sem=x_recv.at[lax.rem(nh - i, nh) * 2 + low, r],
+            device_id={"vel": lax.rem(high + i, nh) * 2 + core}, device_id_type=MESH,
+        )
+
+    def take(r, i, core):
+        return pltpu.make_async_remote_copy(
+            src_ref=cells_of(r, core), dst_ref=tiles.at[i * 2 + core, r],
+            send_sem=x_send.at[i * 2 + core, r], recv_sem=x_recv.at[i * 2 + core, r],
+            device_id={"vel": lax.rem(high + i, nh) * 2 + core}, device_id_type=MESH,
+        )
+
+    def give_back(r):
+        return pltpu.make_async_remote_copy(
+            src_ref=back_out.at[r], dst_ref=back_in.at[r],
+            send_sem=back_send.at[r], recv_sem=back_recv.at[r],
             device_id={"vel": sibling}, device_id_type=MESH,
         )
 
@@ -180,10 +164,11 @@
             device_id={"sy": target}, device_id_type=MESH,
         )
 
-    for k in range(chunks):
+    for r in range(tile_rows):
         for i in range(1, nh):
-            to_chip(k, i).start()
-        to_sibling(k).start()
+            for core in range(2):
+                give(r, i, core).start()
+        give(r, 0, 1 - low).start()
 
     def start_weights(i, carry):
         send_weights(i).start()
@@ -198,10 +183,10 @@
         for j in range(per_row):
             rows = slice(j * GROUP, (j + 1) * GROUP)
             lanes = slice(z * HALF, (z + 1) * HALF)
-            row_out[0, rows, lanes] = tiles[
-                vel, (tile_rows - 1) * per_row + j, :, z * NXY + HALF:(z + 1) * NXY
+            row_out[0, rows, lanes] = own[
+                (tile_rows - 1) * per_row + j, :, z * NXY + HALF:(z + 1) * NXY
             ]
-            row_out[1, rows, lanes] = tiles[vel, j, :, z * NXY:z * NXY + HALF]
+            row_out[1, rows, lanes] = own[j, :, z * NXY:z * NXY + HALF]
     row_halo(0).start()
     row_halo(1).start()
     packed = col_out.shape[1]
@@ -209,7 +194,7 @@
     for way, (part, line) in enumerate(((per_row - 1, GROUP - 1), (0, 0))):
         stack = jnp.concatenate(
             [
-                tiles[vel, r * per_row + part, :, z * NXY:(z + 1) * NXY]
+                own[r * per_row + part, :, z * NXY:(z + 1) * NXY]
                 for r in range(tile_rows)
                 for z in range(depth)
             ],
@@ -224,19 +209,22 @@
         col_halo(way).start()
 
     rows, cols = spread.shape
-    first = vel * depth
-    chosen = (
-        lax.broadcasted_iota(jnp.int32, (rows, NVZ), 1)
-        == (lax.broadcasted_iota(jnp.int32, (rows, NVZ), 0) >> 4) + first
+    chip_first = high * 2 * depth
+    plane_row = lax.broadcasted_iota(jnp.int32, (rows, NVZ), 0) >> 4
+    plane_row = jnp.where(
+        plane_row < depth,
+        plane_row + sibling * depth,
+        plane_row - depth + vel * depth,
     )
-    fan = (
-        lax.broadcasted_iota(jnp.int32, (NVZ, cols), 0)
-        == lax.broadcasted_iota(jnp.int32, (NVZ, cols), 1) >> 4
-    )
-    own = jnp.dot(
+    chosen = lax.broadcasted_iota(jnp.int32, (rows, NVZ), 1) == plane_row
+    plane_col = (
+        (lax.broadcasted_iota(jnp.int32, (NVZ, cols), 1) >> 4) + chip_first
+    ) & (NVZ - 1)
+    fan = lax.broadcasted_iota(jnp.int32, (NVZ, cols), 0) == plane_col
+    picked = jnp.dot(
         jnp.where(chosen, 1.0, 0.0).astype(BF16), d_ref[...], preferred_element_type=F32
     ).astype(BF16)
-    wide = jnp.dot(own, jnp.where(fan, 1.0, 0.0).astype(BF16), preferred_element_type=F32)
+    wide = jnp.dot(picked, jnp.where(fan, 1.0, 0.0).astype(BF16), preferred_element_type=F32)
     same = (
         lax.broadcasted_iota(jnp.int32, (rows, cols), 0) & (GROUP - 1)
     ) == (lax.broadcasted_iota(jnp.int32, (rows, cols), 1) & (GROUP - 1))
@@ -253,26 +241,54 @@
     probe = jnp.where(column == 4, square - coarse, probe)
     probes[...] = probe.astype(BF16)
 
-    vz = [(w - (NVZ - 1) / 2.0) * (8.0 / NVZ) for w in range(NVZ)]
-
-    def relax(k):
-        stack = jnp.concatenate(
+    near = 2 * depth
+
+    def depth_speed(q):
+        plane = lax.rem(chip_first + q, NVZ)
+        return (plane.astype(F32) - (NVZ - 1) / 2.0) * (8.0 / NVZ)
+
+    vz = [depth_speed(q) for q in range(NVZ)]
+
+    def stack_of(r, first, last):
+        return jnp.concatenate(
             [
-                tiles[v, k, :, z * NXY:(z + 1) * NXY]
-                for v in range(nvel)
+                tiles[v, r, :, z * NXY:(z + 1) * NXY]
+                for v in range(first, last)
                 for z in range(depth)
             ],
             axis=0,
         )
+
+    def moments(stack, first, last, start):
         sums = jnp.dot(stack, probes[...], preferred_element_type=F32)
-        plain = jnp.zeros((GROUP, 128), F32)
-        first_order = jnp.zeros((GROUP, 128), F32)
-        second_order = jnp.zeros((GROUP, 128), F32)
-        for w in range(NVZ):
-            term = sums[w * GROUP:(w + 1) * GROUP]
+        plain, first_order, second_order = start
+        for q in range(first, last):
+            term = sums[(q - first) * GROUP:(q - first + 1) * GROUP]
             plain = plain + term
-            first_order = first_order + vz[w] * term
-            second_order = second_order + (vz[w] * vz[w]) * term
+            first_order = first_order + vz[q] * term
+            second_order = second_order + (vz[q] * vz[q]) * term
+        return plain, first_order, second_order
+
+    def prepare(r, carry):
+        load_part(r).wait()
+        take(r, 0, 1 - low).wait_recv()
+        stack = stack_of(r, 0, 2)
+        zero = jnp.zeros((GROUP, 128), F32)
+        for index, block in enumerate(moments(stack, 0, near, (zero, zero, zero))):
+            near_sums[r, index] = block
+        near_mix[r] = jnp.dot(
+            spread[:, :near * GROUP], stack, preferred_element_type=F32
+        )
+        return carry
+
+    def relax(r):
+        for i in range(1, nh):
+            for core in range(2):
+                take(r, i, core).wait_recv()
+        stack = stack_of(r, 2, nvel)
+        plain, first_order, second_order = moments(
+            stack, near, NVZ, tuple(near_sums[r, index] for index in range(3))
+        )
 
         def lanes(block, q):
             return jnp.broadcast_to(block[:, q:q + 1], (GROUP, 128))
@@ -303,9 +319,11 @@
         depth_mix = jnp.dot(spread[...], head, preferred_element_type=F32) + jnp.dot(
             spread[...], rest, preferred_element_type=F32
         )
-        mix = jnp.dot(spread[...], stack, preferred_element_type=F32)
-        even = wider(depth_mix, NXY // 128) * jnp.concatenate([plane] * depth, axis=0)
-        mixed[k] = (even - mix).astype(BF16)
+        mix = near_mix[r] + jnp.dot(
+            spread[:, near * GROUP:], stack, preferred_element_type=F32
+        )
+        even = wider(depth_mix, NXY // 128) * jnp.concatenate([plane] * near, axis=0)
+        mixed[r] = (even - mix).astype(BF16)
 
     vx, vy = lane_speeds((1, NXY), 1)
     pace_x, pace_y = jnp.abs(vx), jnp.abs(vy)
@@ -327,7 +345,7 @@
 
                 def row(index, lanes):
                     return jnp.concatenate(
-                        [tiles[vel, index * per_row + j, :, lanes] for j in range(per_row)],
+                        [own[index * per_row + j, :, lanes] for j in range(per_row)],
                         axis=0,
                     ).astype(F32)
 
@@ -367,60 +385,58 @@
             out_sem.at[k],
         )
 
-    def finish(k, carry):
-        collision = lax.dot_general(
-            mixed[k], weights[...], (((1,), (1,)), ((), ())), preferred_element_type=F32
-        )
+    def through_plane(block):
+        return lax.dot_general(
+            block, weights[...], (((1,), (1,)), ((), ())), preferred_element_type=F32
+        )
+
+    def finish(r, core, collision):
+        k = r * per_row + core
         for z in range(depth):
             lanes = slice(z * NXY, (z + 1) * NXY)
             result[k, :, lanes] = (
                 base[k, :, lanes] + RELAX_RATE * collision[z * GROUP:(z + 1) * GROUP]
             ).astype(BF16)
         store(k).start()
+
+    half_rows = depth * GROUP
+
+    def collide(r):
+        back_out[r] = through_plane(mixed[r, :half_rows]).astype(BF16)
+        give_back(r).start()
+        finish(r, low, through_plane(mixed[r, half_rows:]))
+        give_back(r).wait_recv()
+        finish(r, 1 - low, back_in[r].astype(F32))
+
+    lax.fori_loop(0, tile_rows, prepare, 0)
+    own_weights.wait()
+
+    def await_weights(i, carry):
+        take_weights(i).wait_recv()
         return carry
 
-    gate = chunks - 1
-
-    def step(k, carry):
+    def step(r, carry):
+        relax(r)
+
+        @pl.when(r == 0)
+        def _():
+            lax.fori_loop(1, peers, await_weights, 0)
+            swap_weights(half_lanes).start()
+            transport()
+            swap_weights(sib_lanes).wait_recv()
+
+        collide(r)
+        return carry
+
+    lax.fori_loop(0, tile_rows, step, 0)
+
+    for r in range(tile_rows):
         for i in range(1, nh):
-            from_chip(k, i).wait_recv()
-            forward(k, i).start()
-        from_sibling(k).wait_recv()
-        for i in range(1, nh):
-            forwarded(k, i).wait_recv()
-        relax(k)
-
-        @pl.when(k == chunks - 2)
-        def _():
-            own_weights.wait()
-
-            def take(i, c):
-                take_weights(i).wait_recv()
-                return c
-
-            lax.fori_loop(1, peers, take, 0)
-            swap_weights(half_lanes).start()
-
-        @pl.when(k == 2)
-        def _():
-            transport()
-
-        @pl.when(k == gate)
-        def _():
-            swap_weights(sib_lanes).wait_recv()
-
-        lax.fori_loop(
-            jnp.where(k == gate, 0, k), jnp.where(k >= gate, k + 1, k), finish, 0
-        )
-        return carry
-
-    lax.fori_loop(0, chunks, step, 0)
-
+            for core in range(2):
+                give(r, i, core).wait_send()
+        give(r, 0, 1 - low).wait_send()
+        give_back(r).wait_send()
     for k in range(chunks):
-        for i in range(1, nh):
-            to_chip(k, i).wait_send()
-            forward(k, i).wait_send()
-        to_sibling(k).wait_send()
         store(k).wait()
 
     def sent(i, carry):
@@ -452,26 +468,30 @@
         ],
         out_specs=pl.BlockSpec(memory_space=pl.ANY),
         scratch_shapes=[
-            pltpu.VMEM((nvel, chunks, GROUP, width), BF16),
+            pltpu.VMEM((chunks, GROUP, width), BF16),
+            pltpu.VMEM((nvel, tile_rows, GROUP, width), BF16),
             pltpu.VMEM((NXY, NXY), BF16),
             pltpu.VMEM((chunks, GROUP, width), F32),
-            pltpu.VMEM((chunks, GROUP * depth, NXY), BF16),
+            pltpu.VMEM((tile_rows, 2 * GROUP * depth, NXY), BF16),
             pltpu.VMEM((chunks, GROUP, width), BF16),
-            pltpu.VMEM((GROUP * depth, GROUP * NVZ), BF16),
+            pltpu.VMEM((2 * GROUP * depth, GROUP * NVZ), BF16),
             pltpu.VMEM((NXY, 128), BF16),
+            pltpu.VMEM((tile_rows, 2 * GROUP * depth, NXY), F32),
+            pltpu.VMEM((tile_rows, 3, GROUP, 128), F32),
+            pltpu.VMEM((tile_rows, GROUP * depth, NXY), BF16),
+            pltpu.VMEM((tile_rows, GROUP * depth, NXY), BF16),
             pltpu.VMEM((2, tile_cols, depth * HALF), BF16),
             pltpu.VMEM((2, tile_cols, depth * HALF), BF16),
             pltpu.VMEM((2, packed, NXY), BF16),
             pltpu.VMEM((2, packed, NXY), BF16),
             pltpu.VMEM((2, packed, NXY), F32),
             dma((chunks,)),
+            dma((tile_rows,)),
             dma,
-            dma((nvel // 2, chunks)),
-            dma((nvel // 2, chunks)),
-            dma((chunks,)),
-            dma((chunks,)),
-            dma((nvel // 2, chunks)),
-            dma((nvel // 2, chunks)),
+            dma((nvel, tile_rows)),
+            dma((nvel, tile_rows)),
+            dma((tile_rows,)),
+            dma((tile_rows,)),
             dma((nsx * nsy,)),
             dma((nsx * nsy,)),
             dma((2,)),

time: 54.3 us -> 49.4 us (0.910)
  Pallas kernels: 51.4 us -> 46.5 us
    pallas_call x1, Pallas kernels: 51.4 us -> 46.5 us  [local(): pl.pallas_call(functools.partial(kernel, sizes), out_shape=jax.ShapeDtype...]
where the time goes in v1:
time: 49.4 us; the launch traced here: 49.2 us
  Pallas kernels  46.5 us (94%)
  local copies, waits for them, and re-layouts  2.65 us (5%)
    pallas_call x1, Pallas kernels, local(): pl.pallas_call(functools.partial(kernel, sizes), out_shape=jax.ShapeDtype...  46.5 us
    unnamed x1, local copies, waits for them, and re-layouts  2.65 us

profile of v1, /device:TPU:0, one launch (start us, length us, event | category | flops | bytes accessed | tf_op | source)
XLA Modules:
  0.0 49.2 jit_solution(18402165720474866028)
XLA Ops:
  0.0 46.5 %shard_map.37 = bf16[3,32,8192]{2,1,0:T(8,128)(2,1)} custom-call(bf16[3,32,8192]{2,1,0:T(8,128)(2,1)} %f_hbm.1, bf16[128,1024]{1,0:T(8,128)(2,1)} %w_hbm.1, bf16[32,32]{1,0:T(8,128)(2,1)} %d_ref.1), custom_call_target="tpu_custom_call" | custom-call | flops 1610612736 | bytes 3145728 | tf_op jit(solution)/shard_map/pallas_call | solution.py:461
  46.5 2.7 %copy.5 = bf16[3,32,8192]{2,1,0:T(8,128)(2,1)} copy(bf16[3,32,8192]{2,1,0:T(8,128)(2,1)} %shard_map.37) | data formatting | bytes 3145728

commit v2 on v1

--- a/solution.py
+++ b/solution.py
@@ -30,7 +30,7 @@
 
 def kernel(
     sizes, f_hbm, w_hbm, d_ref, out_hbm,
-    own, tiles, weights, base, mixed, result, spread, probes, near_mix, near_sums,
+    own, tiles, weights, turned, base, mixed, result, spread, probes, near_mix, near_sums,
     back_out, back_in,
     row_out, row_in, col_out, col_in, col_wide,
     loc_sem, part_sem, wloc_sem, x_send, x_recv, back_send, back_recv,
@@ -386,9 +386,7 @@
         )
 
     def through_plane(block):
-        return lax.dot_general(
-            block, weights[...], (((1,), (1,)), ((), ())), preferred_element_type=F32
-        )
+        return jnp.dot(block, turned[...], preferred_element_type=F32)
 
     def finish(r, core, collision):
         k = r * per_row + core
@@ -424,6 +422,7 @@
             swap_weights(half_lanes).start()
             transport()
             swap_weights(sib_lanes).wait_recv()
+            turned[...] = weights[...].T
 
         collide(r)
         return carry
@@ -470,6 +469,7 @@
         scratch_shapes=[
             pltpu.VMEM((chunks, GROUP, width), BF16),
             pltpu.VMEM((nvel, tile_rows, GROUP, width), BF16),
+            pltpu.VMEM((NXY, NXY), BF16),
             pltpu.VMEM((NXY, NXY), BF16),
             pltpu.VMEM((chunks, GROUP, width), F32),
             pltpu.VMEM((tile_rows, 2 * GROUP * depth, NXY), BF16),
@@ -500,7 +500,7 @@
             dma((chunks,)),
         ],
         compiler_params=pltpu.CompilerParams(
-            collective_id=0, has_side_effects=True, vmem_limit_bytes=56 * 1024 * 1024
+            collective_id=0, has_side_effects=True, vmem_limit_bytes=40 * 1024 * 1024
         ),
         cost_estimate=pl.CostEstimate(
             flops=2 * cells * depth * NXY * NXY,

time: 49.4 us -> 49.1 us (level)
  Pallas kernels: 46.5 us -> 44.6 us
  local copies, waits for them, and re-layouts: 2.65 us -> 4.2 us
    pallas_call x1, Pallas kernels: 46.5 us -> 44.6 us  [local(): pl.pallas_call(functools.partial(kernel, sizes), out_shape=jax.ShapeDtype...]
    unnamed x1 -> x7, local copies, waits for them, and re-layouts: 2.65 us -> 4.2 us
where the time goes in v2:
time: 49.1 us; the launch traced here: 48.9 us
  Pallas kernels  44.6 us (91%)
  local copies, waits for them, and re-layouts  4.2 us (9%)
    pallas_call x1, Pallas kernels, local(): pl.pallas_call(functools.partial(kernel, sizes), out_shape=jax.ShapeDtype...  44.6 us
    unnamed x7, local copies, waits for them, and re-layouts  4.2 us

profile of v2, /device:TPU:0, one launch (start us, length us, event | category | flops | bytes accessed | tf_op | source)
XLA Modules:
  0.0 48.9 jit_solution(3606505788601672753)
XLA Ops:
  0.0 0.0 copy-start
  0.0 1.4 %copy-done = bf16[3,32,8192]{2,1,0:T(8,128)(2,1)S(1)} copy-done((bf16[3,32,8192]{2,1,0:T(8,128)(2,1)S(1)}, bf16[3,32,8192]{2,1,0:T(8,128)(2,1)}, u32[]{:S(2)}) %copy-start) | copy-done | bytes 1572888
  1.4 0.0 copy-start.1
  1.4 0.9 %copy-done.1 = bf16[128,1024]{1,0:T(8,128)(2,1)S(1)} copy-done((bf16[128,1024]{1,0:T(8,128)(2,1)S(1)}, bf16[128,1024]{1,0:T(8,128)(2,1)}, u32[]{:S(2)}) %copy-start.1) | copy-done | bytes 262168
  2.4 0.0 copy-start.2
  2.4 0.7 %copy-done.2 = bf16[32,32]{1,0:T(8,128)(2,1)S(1)} copy-done((bf16[32,32]{1,0:T(8,128)(2,1)S(1)}, bf16[32,32]{1,0:T(8,128)(2,1)}, u32[]{:S(2)}) %copy-start.2) | copy-done | bytes 2072
  3.1 44.6 %shard_map.37 = bf16[3,32,8192]{2,1,0:T(8,128)(2,1)S(1)} custom-call(bf16[3,32,8192]{2,1,0:T(8,128)(2,1)S(1)} %copy-done, bf16[128,1024]{1,0:T(8,128)(2,1)S(1)} %copy-done.1, bf16[32,32]{1,0:T(8,128)(2,1)S(1)} %copy-done.2), custom_call_target="tpu_custom_call" | custom-call | flops 1610612736 | bytes 3145728 | tf_op jit(solution)/shard_map/pallas_call | solution.py:460
  47.7 1.1 %copy.5 = bf16[3,32,8192]{2,1,0:T(8,128)(2,1)} copy(bf16[3,32,8192]{2,1,0:T(8,128)(2,1)S(1)} %shard_map.37) | data formatting | bytes 3145728
Async XLA Ops:
  0.0 1.4 %copy-start = (bf16[3,32,8192]{2,1,0:T(8,128)(2,1)S(1)}, bf16[3,32,8192]{2,1,0:T(8,128)(2,1)}, u32[]{:S(2)}) copy-start(bf16[3,32,8192]{2,1,0:T(8,128)(2,1)} %f_hbm.1) | copy-start | bytes 4718596
  1.4 0.9 %copy-start.1 = (bf16[128,1024]{1,0:T(8,128)(2,1)S(1)}, bf16[128,1024]{1,0:T(8,128)(2,1)}, u32[]{:S(2)}) copy-start(bf16[128,1024]{1,0:T(8,128)(2,1)} %w_hbm.1) | copy-start | bytes 786436
  2.4 0.7 %copy-start.2 = (bf16[32,32]{1,0:T(8,128)(2,1)S(1)}, bf16[32,32]{1,0:T(8,128)(2,1)}, u32[]{:S(2)}) copy-start(bf16[32,32]{1,0:T(8,128)(2,1)} %d_ref.1) | copy-start | bytes 6148

commit v3 on v2

--- a/solution.py
+++ b/solution.py
@@ -459,7 +459,7 @@
     cells = tile_rows * tile_cols
     return pl.pallas_call(
         functools.partial(kernel, sizes),
-        out_shape=jax.ShapeDtypeStruct(distribution.shape, BF16),
+        out_shape=pltpu.VMEM(distribution.shape, BF16),
         in_specs=[
             pl.BlockSpec(memory_space=pl.ANY),
             pl.BlockSpec(memory_space=pl.ANY),
@@ -500,7 +500,7 @@
             dma((chunks,)),
         ],
         compiler_params=pltpu.CompilerParams(
-            collective_id=0, has_side_effects=True, vmem_limit_bytes=40 * 1024 * 1024
+            collective_id=0, has_side_effects=True, vmem_limit_bytes=56 * 1024 * 1024
         ),
         cost_estimate=pl.CostEstimate(
             flops=2 * cells * depth * NXY * NXY,

time: 49.1 us -> 46.9 us (0.955)
  local copies, waits for them, and re-layouts: 4.2 us -> 1.15 us
  Pallas kernels: 44.6 us -> 45.6 us
    unnamed x7 -> x1, local copies, waits for them, and re-layouts: 4.2 us -> 1.15 us
    pallas_call x1, Pallas kernels: 44.6 us -> 45.6 us  [local(): pl.pallas_call(functools.partial(kernel, sizes), out_shape=pltpu.VMEM(dis...]
where the time goes in v3:
time: 46.9 us; the launch traced here: 46.7 us
  Pallas kernels  45.6 us (97%)
  local copies, waits for them, and re-layouts  1.15 us (2%)
    pallas_call x1, Pallas kernels, local(): pl.pallas_call(functools.partial(kernel, sizes), out_shape=pltpu.VMEM(dis...  45.6 us
    unnamed x1, local copies, waits for them, and re-layouts  1.15 us

profile of v3, /device:TPU:0, one launch (start us, length us, event | category | flops | bytes accessed | tf_op | source)
XLA Modules:
  0.0 46.7 jit_solution(13326275307914200740)
XLA Ops:
  0.0 45.6 %shard_map.37 = bf16[3,32,8192]{2,1,0:T(8,128)(2,1)S(1)} custom-call(bf16[3,32,8192]{2,1,0:T(8,128)(2,1)} %f_hbm.1, bf16[128,1024]{1,0:T(8,128)(2,1)} %w_hbm.1, bf16[32,32]{1,0:T(8,128)(2,1)} %d_ref.1), custom_call_target="tpu_custom_call" | custom-call | flops 1610612736 | bytes 3145728 | tf_op jit(solution)/shard_map/pallas_call | solution.py:460
  45.6 1.1 %copy.5 = bf16[3,32,8192]{2,1,0:T(8,128)(2,1)} copy(bf16[3,32,8192]{2,1,0:T(8,128)(2,1)S(1)} %shard_map.37) | data formatting | bytes 3145728

commit v4 on v3

--- a/solution.py
+++ b/solution.py
@@ -34,7 +34,7 @@
     back_out, back_in,
     row_out, row_in, col_out, col_in, col_wide,
     loc_sem, part_sem, wloc_sem, x_send, x_recv, back_send, back_recv,
-    w_send, w_recv, wf_sem, halo_send, halo_recv, out_sem,
+    w_send, w_recv, wf_sem, halo_send, halo_recv, out_sem, ready_sem,
 ):
     nvel, nsx, nsy = sizes
     nh = nvel // 2
@@ -53,20 +53,24 @@
 
     barrier = pltpu.get_barrier_semaphore()
 
+    order = sy * nsx + sx
+
+    def cells_at(i):
+        return {"sx": lax.rem(i, nsx), "sy": lax.div(i, nsx)}
+
     def greet(i, carry):
-        peer = lax.rem(me + i, peers)
-        pl.semaphore_signal(
-            barrier, inc=1,
-            device_id={"sx": lax.div(peer, nsy), "sy": lax.rem(peer, nsy)},
-            device_id_type=MESH,
-        )
+        pl.semaphore_signal(barrier, inc=1, device_id=cells_at(i), device_id_type=MESH)
+        return carry
+
+    def answer(i, carry):
+        pl.semaphore_signal(ready_sem, inc=1, device_id=cells_at(i), device_id_type=MESH)
         return carry
 
     for i in range(1, nvel):
         pl.semaphore_signal(
             barrier, inc=1, device_id={"vel": lax.rem(vel + i, nvel)}, device_id_type=MESH
         )
-    lax.fori_loop(1, peers, greet, 0)
+    lax.fori_loop(order + 1, peers, greet, 0)
 
     def piece(k):
         return f_hbm.at[
@@ -98,7 +102,7 @@
     for r in range(tile_rows):
         load_part(r).start()
     own_weights.start()
-    pl.semaphore_wait(barrier, peers + nvel - 2)
+    pl.semaphore_wait(barrier, nvel - 1 + order)
 
     def give(r, i, core):
         return pltpu.make_async_remote_copy(
@@ -173,6 +177,12 @@
     def start_weights(i, carry):
         send_weights(i).start()
         return carry
+
+    lax.fori_loop(0, order, answer, 0)
+
+    @pl.when(order < peers - 1)
+    def _():
+        pl.semaphore_wait(ready_sem, peers - 1 - order)
 
     lax.fori_loop(1, peers, start_weights, 0)
 
@@ -498,6 +508,7 @@
             dma((4,)),
             dma((4,)),
             dma((chunks,)),
+            pltpu.SemaphoreType.REGULAR,
         ],
         compiler_params=pltpu.CompilerParams(
             collective_id=0, has_side_effects=True, vmem_limit_bytes=56 * 1024 * 1024

time: 46.9 us -> 45.2 us (0.964)
  the two profiles are of different devices: /device:TPU:0 before, /device:TPU:9 now
where the time goes in v4:
time: 45.2 us; the launch traced here: 45 us
  Pallas kernels  43.9 us (97%)
  local copies, waits for them, and re-layouts  1.15 us (3%)
    pallas_call x1, Pallas kernels, local(): pl.pallas_call(functools.partial(kernel, sizes), out_shape=pltpu.VMEM(dis...  43.9 us
    unnamed x1, local copies, waits for them, and re-layouts  1.15 us

profile of v4, /device:TPU:9, one launch (start us, length us, event | category | flops | bytes accessed | tf_op | source)
XLA Modules:
  0.0 45.0 jit_solution(13681903462988578601)
XLA Ops:
  0.0 43.9 %shard_map.37 = bf16[3,32,8192]{2,1,0:T(8,128)(2,1)S(1)} custom-call(bf16[3,32,8192]{2,1,0:T(8,128)(2,1)} %f_hbm.1, bf16[128,1024]{1,0:T(8,128)(2,1)} %w_hbm.1, bf16[32,32]{1,0:T(8,128)(2,1)} %d_ref.1), custom_call_target="tpu_custom_call" | custom-call | flops 1610612736 | bytes 3145728 | tf_op jit(solution)/shard_map/pallas_call | solution.py:470
  43.9 1.1 %copy.5 = bf16[3,32,8192]{2,1,0:T(8,128)(2,1)} copy(bf16[3,32,8192]{2,1,0:T(8,128)(2,1)S(1)} %shard_map.37) | data formatting | bytes 3145728
